TPU v7x, 128 devices: a whole 4x4x4 slice. The times are simulated.
128 devices in a mesh: seq: 8 (over x, core), head: 16 (over z, y).
Axes of the slice: x: 4, y: 4, z: 4, core: 2. Of those that a mesh axis runs over, the one named last changes fastest.
Arguments:
- tokens: bfloat16 [1024, 6144], P('seq'), may hold values from -6 to 6
- log_decay: float32 [1024, 32], P('seq', 'head'), may hold values from -1 to 0
- carried_state: float32 [32, 128, 128], P('head'), may hold values from -48 to 48
- q_weight: bfloat16 [6144, 4096], P(None, 'head'), may hold values from -0.078125 to 0.078125
- k_weight: bfloat16 [6144, 4096], P(None, 'head'), may hold values from -0.078125 to 0.078125
- v_weight: bfloat16 [6144, 4096], P(None, 'head'), may hold values from -0.078125 to 0.078125
- out_weight: bfloat16 [4096, 6144], P('head'), may hold values from -0.09375 to 0.09375
- final_gain: bfloat16 [6144], replicated, may hold values from 0.099609375 to 1.8984375
- vocab_weight: bfloat16 [6144, 131072], P(None, ('seq', 'head')), may hold values from -5 to 5
- targets: int32 [1024], replicated, may hold values from 0 to 131071
Outputs:
- loglik: float32 [1024], P('seq')
All inputs are finite; a program needn't handle non-finite values.
Results may differ from a plain program's by a relative error of at most 0.002.
Values may be sent and summed in bfloat16 or wider, within the bound.
No kernel may reach another device: no remote copies, remote signals or barrier semaphores. Data moves between devices by JAX's collectives and lax.ppermute only.
A program may use at most 128 MiB of HBM per device.

v0:
```python
import jax
import jax.numpy as jnp
from jax import lax
from jax.sharding import PartitionSpec as P


def prefix(array, axis, combine, identity):
    length, here = (lax.axis_size(axis), lax.axis_index(axis))
    everything = jax.tree.map(lambda part: lax.all_gather(part, axis), array)
    start = jax.tree.map(
        lambda part, zero: jnp.broadcast_to(jnp.asarray(zero, part.dtype), part.shape),
        array,
        identity,
    )

    def turn(k, before):
        reached = k < here
        new = combine(before, jax.tree.map(lambda part: part[k], everything))
        return jax.tree.map(lambda a, b: jnp.where(reached, a, b), new, before)

    return lax.fori_loop(0, length, turn, start)


def combine_states(earlier, later):
    return (earlier[0] * later[0], later[0][:, None, None] * earlier[1] + later[1])


def shards(
    tokens,
    log_decay,
    carried_state,
    q_weight,
    k_weight,
    v_weight,
    out_weight,
    final_gain,
    vocab_weight,
    targets,
):
    highest = lax.Precision.HIGHEST
    rows_here = tokens.shape[0]
    heads_here = carried_state.shape[0]
    head_size = carried_state.shape[1]
    view = (rows_here, heads_here, head_size)
    queries = (
        jnp.dot(tokens, q_weight, preferred_element_type=jnp.float32)
        .astype(jnp.bfloat16)
        .reshape(view)
    )
    keys_loc = (
        jnp.dot(tokens, k_weight, preferred_element_type=jnp.float32)
        .astype(jnp.bfloat16)
        .reshape(view)
    )
    values = (
        jnp.dot(tokens, v_weight, preferred_element_type=jnp.float32)
        .astype(jnp.bfloat16)
        .reshape(view)
    )
    cumul = jnp.cumsum(log_decay, axis=0)
    last_cum = cumul[-1]
    ends = jnp.exp(last_cum[None, :] - cumul)
    local_state = jnp.einsum(
        "thd,the->hde",
        keys_loc.astype(jnp.float32) * ends[:, :, None],
        values.astype(jnp.float32),
        precision=highest,
    )
    total_decay = jnp.exp(last_cum)
    prefix_decay, prefix_state = prefix(
        (total_decay, local_state),
        "seq",
        combine_states,
        (jnp.ones_like(total_decay), jnp.zeros_like(local_state)),
    )
    lower = jnp.arange(rows_here)[:, None] >= jnp.arange(rows_here)[None, :]
    scores = jnp.einsum("thd,shd->hts", queries, keys_loc, preferred_element_type=jnp.float32)
    diff = jnp.transpose(cumul[:, None, :] - cumul[None, :, :], (2, 0, 1))
    weight = (scores * jnp.exp(jnp.where(lower[None], diff, -1e30))).astype(jnp.bfloat16)
    intra = jnp.einsum("hts,shd->thd", weight, values, preferred_element_type=jnp.float32)
    state_in = prefix_decay[:, None, None] * carried_state + prefix_state
    inter = jnp.exp(cumul)[:, :, None] * jnp.einsum(
        "thd,hde->the", queries.astype(jnp.float32), state_in, precision=highest
    )
    attended = intra + inter
    normed_heads = attended * lax.rsqrt(
        jnp.mean(attended * attended, axis=-1, keepdims=True) + 1e-06
    )
    flat_heads = normed_heads.astype(jnp.bfloat16).reshape(rows_here, heads_here * head_size)
    rows_mine = rows_here // lax.axis_size("head")
    head_index = lax.axis_index("head")
    mixed_all = lax.psum(
        jnp.dot(flat_heads, out_weight, preferred_element_type=jnp.float32), "head"
    )
    mixed = lax.dynamic_slice_in_dim(mixed_all, head_index * rows_mine, rows_mine, 0)
    resid = (
        lax.dynamic_slice_in_dim(tokens, head_index * rows_mine, rows_mine, 0).astype(jnp.float32)
        + mixed
    )
    final_rows = (
        resid
        * lax.rsqrt(jnp.mean(resid * resid, axis=-1, keepdims=True) + 1e-06)
        * final_gain.astype(jnp.float32)
    )
    final_rows = final_rows.astype(jnp.bfloat16)
    vocab_local = vocab_weight.shape[1]
    offset = (lax.axis_index("seq") * lax.axis_size("head") + head_index) * vocab_local
    columns = jnp.arange(vocab_local, dtype=jnp.int32)
    logits = jnp.dot(
        lax.all_gather(final_rows, ("seq", "head"), axis=0, tiled=True),
        vocab_weight,
        preferred_element_type=jnp.float32,
    )
    top = jnp.max(logits, axis=1)
    total = jnp.sum(jnp.exp(logits - top[:, None]), axis=1)
    wanted = targets - offset
    hit = jnp.sum(jnp.where(columns[None, :] == wanted[:, None], logits, 0.0), axis=1)
    top_all = lax.pmax(top, ("seq", "head"))
    total_all, hit_all = lax.psum((total * jnp.exp(top - top_all), hit), ("seq", "head"))
    loglik = hit_all - top_all - jnp.log(total_all)
    return lax.dynamic_slice_in_dim(loglik, lax.axis_index("seq") * rows_here, rows_here, 0)


def solution(mesh):
    return jax.shard_map(
        shards,
        mesh=mesh,
        in_specs=(
            P("seq", None),
            P("seq", "head"),
            P("head", None, None),
            P(None, "head"),
            P(None, "head"),
            P(None, "head"),
            P("head", None),
            P(),
            P(None, ("seq", "head")),
            P(),
        ),
        out_specs=P("seq"),
        check_vma=False,
    )
```

profile of v0, /device:TPU:1, one launch (start us, length us, event | category | flops | bytes accessed | tf_op | source)
XLA Modules:
  0.0 385.3 jit_solution(14718534888018662489)
XLA Ops:
  6.5 0.0 copy-start
  6.5 0.0 all-gather.7.cloned.1.call-start
  6.5 0.9 copy.23
  7.5 0.2 reduce_window_sum.11
  7.7 0.1 copy.30
  7.7 3.0 convolution_convert_fusion
  10.7 0.1 copy.36
  10.8 3.0 fusion.4
  13.8 0.9 fusion.8
  14.6 0.0 all-gather.7.cloned.1.call-update
  14.7 0.0 all-reduce.3.cloned.1.call-start
  14.7 11.8 %all-gather.1 = f32[8,1,2]{2,1,0:T(1,128)S(1)} all-gather(f32[1,1,2]{2,1,0:T(1,128)S(1)} %get-tuple-element.171), channel_id=1, replica_groups=mesh['seq'=8,'head'=16] {'seq'}, dimensions={0}, use_global_device_ids=true | all-gather | bytes 72 | tf_op jit(solution)/shard_map/all_gather | solution.py:9
  26.5 0.1 copy.27
  26.6 0.1 copy.24
  26.7 3.1 fusion.5
  29.8 12.0 %all-gather.7.cloned.1.call-done = f32[16,128,128]{2,1,0:T(8,128)} async-done(((f32[2,128,128]{2,1,0:T(8,128)}), f32[16,128,128]{2,1,0:T(8,128)}) %all-gather.7.cloned.1.call-update) | async-done | bytes 1048592 | tf_op jit(solution)/shard_map/all_gather | solution.py:9
  41.8 8.3 %while.16 = (s32[]{:T(128)}, f32[2]{0:T(128)S(1)}, f32[2,128,128]{2,1,0:T(8,128)S(1)}, s32[]{:T(128)}, f32[8,2]{1,0:T(8,128)S(1)}, /*index=5*/f32[8,2,128,128]{3,2,1,0:T(8,128)}, s32[]{:T(128)}, s32[]{:T(128)}) while((s32[]{:T(128)}, f32[2]{0:T(128)S(1)}, f32[2,128,128]{2,1,0:T(8,128)S(1)}, s32[]{:T(128)}, f32[8,2]{1,0:T(8,128)S(1)}, ...), condition=%wide.region_2.3_spmd.clone, body=%wide.region_1.2_spmd.clone.sunk | while | flops 131082 | bytes 393371 | solution.py:21
  41.8 1.0 fusion.48
  42.8 1.0 fusion.48
  43.9 1.0 fusion.48
  44.9 1.0 fusion.48
  46.0 1.0 fusion.48
  47.0 1.0 fusion.48
  48.0 1.0 fusion.48
  49.1 1.0 fusion.48
  50.1 1.9 fusion.1
  52.0 1.2 multiply_reduce_fusion.1
  53.3 0.0 copy-done
  53.3 2.3 fusion.35
  55.6 0.0 copy-start.1
  55.6 0.0 copy-start.2
  55.6 0.0 all-reduce.3.cloned.1.call-update
  55.6 0.0 all-gather.5.cloned.1.call-start
  55.7 0.6 copy-done.1
  56.3 94.3 %all-reduce.3.cloned.1.call-done = f32[128,6144]{1,0:T(8,128)} async-done(((f32[128,6144]{1,0:T(8,128)}), f32[128,6144]{1,0:T(8,128)}) %all-reduce.3.cloned.1.call-update) | async-done | bytes 3145744 | tf_op jit(solution)/shard_map/psum | solution.py:92
  150.6 1.2 multiply_reduce_fusion
  151.8 1.7 multiply_convert_fusion
  153.5 0.0 all-gather.5.cloned.1.call-update
  153.5 0.0 copy-done.2
  153.6 73.3 %all-gather.5.cloned.1.call-done = bf16[1024,6144]{1,0:T(8,128)(2,1)} async-done(((bf16[8,6144]{1,0:T(8,128)(2,1)}), bf16[1024,6144]{1,0:T(8,128)(2,1)}) %all-gather.5.cloned.1.call-update) | async-done | bytes 12582928 | tf_op jit(solution)/shard_map/all_gather | solution.py:110
  226.9 19.4 %fusion.34 = (f32[1024]{0:T(1024)S(1)}, f32[1024,1024]{0,1:T(8,128)}) fusion(bf16[1024,6144]{1,0:T(8,128)(2,1)} %all-gather.5.cloned.1.call-done, bf16[6144,1024]{1,0:T(8,128)(2,1)} %param.20), kind=kOutput, calls=%fused_computation.57 | convolution fusion | flops 12885949440 | bytes 29364224 | tf_op jit(solution)/shard_map/dot_general | solution.py:109
  246.3 64.4 %pmax.7 = f32[1024]{0:T(1024)S(1)} all-reduce(f32[1024]{0:T(1024)S(1)} %get-tuple-element.174), channel_id=1, replica_groups=mesh['seq'=8,'head'=16] {'seq','head'}, use_global_device_ids=true, to_apply=%region_9.10 | all-reduce | flops 1024 | bytes 8192 | tf_op jit(solution)/shard_map/pmax | solution.py:118
  310.7 3.3 select_reduce_fusion
  314.0 64.2 %all-reduce = (f32[1024]{0:T(1024)S(1)}, f32[1024]{0:T(1024)S(1)}) all-reduce(f32[1024]{0:T(1024)S(1)} %exponential_multiply_fusion, f32[1024]{0:T(1024)S(1)} %get-tuple-element.150), channel_id=1, replica_groups=mesh['seq'=8,'head'=16] {'seq','head'}, use_global_device_ids=true, to_apply=%region_11.12 | all-reduce | flops 2048 | bytes 16384 | tf_op jit(solution)/shard_map/psum | solution.py:119
  378.2 0.6 dynamic_slice.25
  (20 shorter events, 0.3 us)
Async XLA Ops:
  6.5 46.7 %copy-start = (bf16[256,6144]{1,0:T(8,128)(2,1)S(1)}, bf16[256,6144]{1,0:T(8,128)(2,1)}, u32[]{:S(2)}) copy-start(bf16[256,6144]{1,0:T(8,128)(2,1)} %param.18) | copy-start | bytes 9437188
  6.5 35.2 %all-gather.7.cloned.1.call-start = ((), (), s32[]{:S(2)}) async-start(), calls=%async_computation.2 | async-start | bytes 1179648 | tf_op jit(solution)/shard_map/all_gather | solution.py:9
  14.7 135.9 %all-reduce.3.cloned.1.call-start = ((), (), s32[]{:S(2)}) async-start(), calls=%async_computation | async-start | bytes 6291456 | tf_op jit(solution)/shard_map/psum | solution.py:92
  55.6 0.7 copy-start.1
  55.6 98.0 %copy-start.2 = (s32[1024]{0:T(1024)S(1)}, s32[1024]{0:T(1024)}, u32[]{:S(2)}) copy-start(s32[1024]{0:T(1024)} %param.21) | copy-start | bytes 12292
  55.6 171.3 %all-gather.5.cloned.1.call-start = ((), (), s32[]{:S(2)}) async-start(), calls=%async_computation.1 | async-start | bytes 12681216 | tf_op jit(solution)/shard_map/all_gather | solution.py:110
Sparse Core Ops, SparseCore 0:
  14.8 26.9 all-gather.6
  55.7 94.8 all-reduce.2
  153.7 73.0 all-gather.4
where the time goes:
time: 386 us; the launch traced here: 385 us
  waiting for transfers between devices  180 us (47%)
  blocking collectives  140 us (36%)
  matrix products  34.7 us (9%)
  other arithmetic  14.5 us (4%)
  between operations  13.2 us (3%)
    psum x1, waiting for transfers between devices, shards(): lax.psum(jnp.dot(flat_heads, out_weight, preferred_element_type=jnp.float...  94.3 us
    all_gather x1, waiting for transfers between devices, shards(): lax.all_gather(final_rows, ('seq', 'head'), axis=0, tiled=True)  73.3 us
    pmax x1, blocking collectives, shards(): top_all = lax.pmax(top, ('seq', 'head'))  64.4 us
    psum x1, blocking collectives, shards(): lax.psum((total * jnp.exp(top - top_all), hit), ('seq', 'head'))  64.2 us
    dot_general x1, matrix products, shards(): jnp.dot(lax.all_gather(final_rows, ('seq', 'head'), axis=0, tiled=True),...  19.4 us
    all_gather x1, waiting for transfers between devices, prefix(): everything = jax.tree.map(lambda part: lax.all_gather(part, axis), array)  12 us
    all_gather x1, blocking collectives, prefix(): everything = jax.tree.map(lambda part: lax.all_gather(part, axis), array)  11.8 us
    select_n x16, other arithmetic, turn(): return jax.tree.map(lambda a, b: jnp.where(reached, a, b), new, before)  8.09 us
  transfers between devices with their start and end apart: 3, of which 3 were waited for; matrix products, arithmetic and copies ran while one was open for 1% of the time, Pallas kernels for 0%

commit v1 on v0

--- a/solution.py
+++ b/solution.py
@@ -116,7 +116,7 @@
     wanted = targets - offset
     hit = jnp.sum(jnp.where(columns[None, :] == wanted[:, None], logits, 0.0), axis=1)
     top_all = lax.pmax(top, ("seq", "head"))
-    total_all, hit_all = lax.psum((total * jnp.exp(top - top_all), hit), ("seq", "head"))
+    total_all, hit_all = lax.psum(lax.psum((total * jnp.exp(top - top_all), hit), "seq"), "head")
     loglik = hit_all - top_all - jnp.log(total_all)
     return lax.dynamic_slice_in_dim(loglik, lax.axis_index("seq") * rows_here, rows_here, 0)
 

time: 386 us -> 373 us (0.966)
  the two profiles are of different devices: /device:TPU:1 before, /device:TPU:0 now
where the time goes in v1:
time: 373 us; the launch traced here: 372 us
  waiting for transfers between devices  180 us (48%)
  blocking collectives  127 us (34%)
  matrix products  34.7 us (9%)
  other arithmetic  14.5 us (4%)
  between operations  13.3 us (4%)
    psum x1, waiting for transfers between devices, shards(): lax.psum(jnp.dot(flat_heads, out_weight, preferred_element_type=jnp.float...  95.3 us
    all_gather x1, waiting for transfers between devices, shards(): lax.all_gather(final_rows, ('seq', 'head'), axis=0, tiled=True)  72.3 us
    pmax x1, blocking collectives, shards(): top_all = lax.pmax(top, ('seq', 'head'))  64.8 us
    psum x1, blocking collectives, shards(): lax.psum(lax.psum((total * jnp.exp(top - top_all), hit), 'seq'), 'head')  37.4 us
    dot_general x1, matrix products, shards(): jnp.dot(lax.all_gather(final_rows, ('seq', 'head'), axis=0, tiled=True),...  19.4 us
    psum x1, blocking collectives, shards(): lax.psum((total * jnp.exp(top - top_all), hit), 'seq')  14.4 us
    all_gather x1, waiting for transfers between devices, prefix(): everything = jax.tree.map(lambda part: lax.all_gather(part, axis), array)  12 us
    all_gather x1, blocking collectives, prefix(): everything = jax.tree.map(lambda part: lax.all_gather(part, axis), array)  10.6 us
  transfers between devices with their start and end apart: 3, of which 3 were waited for; matrix products, arithmetic and copies ran while one was open for 1% of the time, Pallas kernels for 0%

profile of v1, /device:TPU:0, one launch (start us, length us, event | category | flops | bytes accessed | tf_op | source)
XLA Modules:
  0.0 372.2 jit_solution(12764877152304014125)
XLA Ops:
  6.5 0.0 copy-start
  6.5 0.0 all-gather.7.cloned.1.call-start
  6.5 0.9 copy.23
  7.5 0.2 reduce_window_sum.11
  7.7 0.1 copy.30
  7.7 3.0 convolution_convert_fusion
  10.7 0.1 copy.36
  10.8 2.9 fusion.4
  13.8 0.9 fusion.8
  14.6 0.0 all-gather.7.cloned.1.call-update
  14.7 0.0 all-reduce.4.cloned.1.call-start
  14.7 10.6 %all-gather.1 = f32[8,1,2]{2,1,0:T(1,128)S(1)} all-gather(f32[1,1,2]{2,1,0:T(1,128)S(1)} %get-tuple-element.173), channel_id=1, replica_groups=mesh['seq'=8,'head'=16] {'seq'}, dimensions={0}, use_global_device_ids=true | all-gather | bytes 72 | tf_op jit(solution)/shard_map/all_gather | solution.py:9
  25.3 0.1 copy.27
  25.4 0.1 copy.24
  25.5 3.1 fusion.5
  28.6 12.0 %all-gather.7.cloned.1.call-done = f32[16,128,128]{2,1,0:T(8,128)} async-done(((f32[2,128,128]{2,1,0:T(8,128)}), f32[16,128,128]{2,1,0:T(8,128)}) %all-gather.7.cloned.1.call-update) | async-done | bytes 1048592 | tf_op jit(solution)/shard_map/all_gather | solution.py:9
  40.6 8.3 %while.16 = (s32[]{:T(128)}, f32[2]{0:T(128)S(1)}, f32[2,128,128]{2,1,0:T(8,128)S(1)}, s32[]{:T(128)}, f32[8,2]{1,0:T(8,128)S(1)}, /*index=5*/f32[8,2,128,128]{3,2,1,0:T(8,128)}, s32[]{:T(128)}, s32[]{:T(128)}) while((s32[]{:T(128)}, f32[2]{0:T(128)S(1)}, f32[2,128,128]{2,1,0:T(8,128)S(1)}, s32[]{:T(128)}, f32[8,2]{1,0:T(8,128)S(1)}, ...), condition=%wide.region_2.3_spmd.clone, body=%wide.region_1.2_spmd.clone.sunk | while | flops 131082 | bytes 393371 | solution.py:21
  40.6 1.0 fusion.48
  41.7 1.0 fusion.48
  42.7 1.0 fusion.48
  43.7 1.0 fusion.48
  44.8 1.0 fusion.48
  45.8 1.0 fusion.48
  46.9 1.0 fusion.48
  47.9 1.0 fusion.48
  48.9 1.9 fusion.1
  50.8 1.2 multiply_reduce_fusion.1
  52.1 0.0 copy-done
  52.1 2.3 fusion.35
  54.4 0.0 copy-start.1
  54.4 0.0 copy-start.2
  54.4 0.0 all-reduce.4.cloned.1.call-update
  54.4 0.0 all-gather.5.cloned.1.call-start
  54.5 0.6 copy-done.1
  55.1 95.3 %all-reduce.4.cloned.1.call-done = f32[128,6144]{1,0:T(8,128)} async-done(((f32[128,6144]{1,0:T(8,128)}), f32[128,6144]{1,0:T(8,128)}) %all-reduce.4.cloned.1.call-update) | async-done | bytes 3145744 | tf_op jit(solution)/shard_map/psum | solution.py:92
  150.4 1.2 multiply_reduce_fusion
  151.6 1.7 multiply_convert_fusion
  153.3 0.0 all-gather.5.cloned.1.call-update
  153.3 0.0 copy-done.2
  153.3 72.3 %all-gather.5.cloned.1.call-done = bf16[1024,6144]{1,0:T(8,128)(2,1)} async-done(((bf16[8,6144]{1,0:T(8,128)(2,1)}), bf16[1024,6144]{1,0:T(8,128)(2,1)}) %all-gather.5.cloned.1.call-update) | async-done | bytes 12582928 | tf_op jit(solution)/shard_map/all_gather | solution.py:110
  225.7 19.4 %fusion.34 = (f32[1024]{0:T(1024)S(1)}, f32[1024,1024]{0,1:T(8,128)}) fusion(bf16[1024,6144]{1,0:T(8,128)(2,1)} %all-gather.5.cloned.1.call-done, bf16[6144,1024]{1,0:T(8,128)(2,1)} %param.20), kind=kOutput, calls=%fused_computation.57 | convolution fusion | flops 12885949440 | bytes 29364224 | tf_op jit(solution)/shard_map/dot_general | solution.py:109
  245.1 64.8 %pmax.7 = f32[1024]{0:T(1024)S(1)} all-reduce(f32[1024]{0:T(1024)S(1)} %get-tuple-element.176), channel_id=1, replica_groups=mesh['seq'=8,'head'=16] {'seq','head'}, use_global_device_ids=true, to_apply=%region_10.11 | all-reduce | flops 1024 | bytes 8192 | tf_op jit(solution)/shard_map/pmax | solution.py:118
  309.9 3.3 select_reduce_fusion
  313.2 14.4 %all-reduce.1 = (f32[1024]{0:T(1024)S(1)}, f32[1024]{0:T(1024)S(1)}) all-reduce(f32[1024]{0:T(1024)S(1)} %exponential_multiply_fusion, f32[1024]{0:T(1024)S(1)} %get-tuple-element.150), channel_id=1, replica_groups=mesh['seq'=8,'head'=16] {'seq'}, use_global_device_ids=true, to_apply=%region_12.13 | all-reduce | flops 2048 | bytes 16384 | tf_op jit(solution)/shard_map/psum | solution.py:119
  327.6 37.4 %all-reduce = (f32[1024]{0:T(1024)S(1)}, f32[1024]{0:T(1024)S(1)}) all-reduce(f32[1024]{0:T(1024)S(1)} %get-tuple-element.166, f32[1024]{0:T(1024)S(1)} %get-tuple-element.167), channel_id=1, replica_groups=mesh['seq'=8,'head'=16] {'head'}, use_global_device_ids=true, to_apply=%region_13.14 | all-reduce | flops 2048 | bytes 16384 | tf_op jit(solution)/shard_map/psum | solution.py:119
  365.1 0.6 dynamic_slice.25
  (20 shorter events, 0.3 us)
Async XLA Ops:
  6.5 45.5 %copy-start = (bf16[256,6144]{1,0:T(8,128)(2,1)S(1)}, bf16[256,6144]{1,0:T(8,128)(2,1)}, u32[]{:S(2)}) copy-start(bf16[256,6144]{1,0:T(8,128)(2,1)} %param.18) | copy-start | bytes 9437188
  6.5 34.1 %all-gather.7.cloned.1.call-start = ((), (), s32[]{:S(2)}) async-start(), calls=%async_computation.2 | async-start | bytes 1179648 | tf_op jit(solution)/shard_map/all_gather | solution.py:9
  14.7 135.7 %all-reduce.4.cloned.1.call-start = ((), (), s32[]{:S(2)}) async-start(), calls=%async_computation | async-start | bytes 6291456 | tf_op jit(solution)/shard_map/psum | solution.py:92
  54.4 0.7 copy-start.1
  54.4 98.9 %copy-start.2 = (s32[1024]{0:T(1024)S(1)}, s32[1024]{0:T(1024)}, u32[]{:S(2)}) copy-start(s32[1024]{0:T(1024)} %param.21) | copy-start | bytes 12292
  54.4 171.3 %all-gather.5.cloned.1.call-start = ((), (), s32[]{:S(2)}) async-start(), calls=%async_computation.1 | async-start | bytes 12681216 | tf_op jit(solution)/shard_map/all_gather | solution.py:110
Sparse Core Ops, SparseCore 0:
  14.8 25.7 all-gather.6
  54.5 95.8 all-reduce.3
  153.5 72.1 all-gather.4
